TPU v7x, 32 devices: a whole 2x2x4 slice. The times are simulated.
32 devices in a mesh: seq: 8 (over z, y), exp: 4 (over x, core).
Axes of the slice: x: 2, y: 2, z: 4, core: 2. Of those that a mesh axis runs over, the one named last changes fastest.
Arguments:
- resid_rows: bfloat16 [4, 32, 3072], P('exp', 'seq'), may hold values from -6 to 6
- query_rows: bfloat16 [4, 32, 3072], P('exp', 'seq'), may hold values from -6 to 6
- key_rows: bfloat16 [4, 1024, 3072], P('exp', 'seq'), may hold values from -6 to 6
- value_rows: bfloat16 [4, 1024, 3072], P('exp', 'seq'), may hold values from -6 to 6
- log_decay: float32 [4, 48, 1024], P('exp', None, 'seq'), may hold values from -1 to 0
- read_pos: int32 [4, 32], P('exp', 'seq'), may hold values from 0 to 1023, as said below
- expert_ids: int32 [4, 32, 2], P('exp', 'seq'), may hold values from 0 to 3, all different within a row; in each aligned block of 4 rows (0 to 3, 4 to 7, ..., all dimensions but the last counted through in order) at most 4 rows name the same one
- pair_order: int32 [4], replicated, may hold values from 0 to 3, each once
- lengths: int32 [4], replicated, may hold values from 1 to 1024
- norm_gain: bfloat16 [3072], replicated, may hold values from 0.5 to 1.5
- router_weight: bfloat16 [3072, 4], replicated, may hold values from -0.109375 to 0.109375
- score_weight: bfloat16 [3072], replicated, may hold values from -0.109375 to 0.109375
- gate_weight: bfloat16 [4, 3072, 9216], P('exp', None, 'seq'), may hold values from -0.109375 to 0.109375
- up_weight: bfloat16 [4, 3072, 9216], P('exp', None, 'seq'), may hold values from -0.109375 to 0.109375
- down_weight: bfloat16 [4, 9216, 3072], P('exp', 'seq'), may hold values from -0.0625 to 0.0625
Outputs:
- pair_loss: float32 [], replicated
- grad_query: float32 [4, 32, 3072], P('exp', 'seq')
- grad_resid: float32 [4, 32, 3072], P('exp', 'seq')
- grad_keys: bfloat16 [4, 1024, 3072], P('exp', 'seq')
- grad_values: bfloat16 [4, 1024, 3072], P('exp', 'seq')
Inputs may be any that keep to these rules, and one draw needn't show every extreme that they name: `read_pos`: each aligned block j of 4 entries of a sequence holds strictly increasing positions from j * 128 to (j + 1) * 128 - 1, the last of them being (j + 1) * 128 - 1. `expert_ids`: the two entries of a row differ; in the rows of one device (aligned blocks of 4 rows) no expert is named by more than 4 rows. `pair_order`: each sequence appears once.
All inputs are finite; a program needn't handle non-finite values.
Results may differ from a plain program's by a relative error of at most 0.018.
Values may be sent and summed in bfloat16 or wider, within the bound.
A program may use at most 128 MiB of HBM per device.

v0:
```python
import jax
import jax.numpy as jnp
from jax import lax
from jax.sharding import PartitionSpec as P

PRECISE = lax.Precision.HIGHEST
EPSILON = 1e-06
LENGTH_WEIGHT = 4.0
SCORE_SCALE = 256.0


def carried_in(value, axis, join, neutral, backward):
    count = lax.axis_size(axis)
    place = lax.axis_index(axis)
    ahead = count - 1 - place if backward else place
    gathered = jax.tree.map(
        lambda a, kind: lax.all_gather(a.astype(kind), axis), value, (jnp.bfloat16, jnp.bfloat16)
    )
    state = jax.tree.map(lambda a, e: jnp.zeros_like(a) + jnp.asarray(e, a.dtype), value, neutral)

    def one(lap, state):
        source = count - 1 - lap if backward else lap
        return join(
            state,
            jax.tree.map(
                lambda a, own: lax.dynamic_index_in_dim(a, source, 0, False).astype(own.dtype),
                gathered,
                value,
            ),
        )

    return lax.fori_loop(0, ahead, one, state)


def merge_states(earlier, later):
    return (earlier[0] * later[0], later[0][:, None, None] * earlier[1] + later[1])


def chain_prefix(decay, summary, backwards):
    blank = (jnp.ones_like(decay), jnp.zeros_like(summary))
    joined = carried_in((decay, summary), "seq", merge_states, blank, backwards)
    return joined[1]


def readout_weights(cumulated, places):
    positions = jnp.arange(cumulated.shape[1], dtype=jnp.int32)
    one_hot = (places[:, None] == positions[None, :]).astype(jnp.float32)
    at_read = jnp.dot(cumulated, one_hot.T, precision=PRECISE)
    allowed = positions[None, :] <= places[:, None]
    exponent = jnp.where(allowed[None], at_read[:, :, None] - cumulated[:, None, :], -1e30)
    return (at_read, jnp.exp(exponent))


def preference_loss(rewards, pair_order, lengths, total_length):
    count = rewards.shape[0]
    ordering = (pair_order[:, None] == jnp.arange(count, dtype=jnp.int32)[None, :]).astype(
        jnp.float32
    )
    ranked = jnp.dot(ordering, rewards, precision=PRECISE).reshape(count // 2, 2)
    fitted = jnp.mean(jax.nn.softplus(ranked[:, 1] - ranked[:, 0]))
    share = lengths.astype(jnp.float32) / total_length
    scatter_breadth = jnp.mean((rewards - jnp.mean(rewards)) * (share - jnp.mean(share)))
    return fitted + LENGTH_WEIGHT * scatter_breadth * scatter_breadth


def to_experts(slots):
    return lax.all_to_all(slots, "exp", split_axis=0, concat_axis=0, tiled=True)


def over_slots(arrived, project):
    return project(lax.all_gather(arrived, "seq", axis=0, tiled=True), jnp.int32(0))


def collect(project, expert_count, capacity):
    slot_count = expert_count * capacity
    summed = lax.psum_scatter(
        project(jnp.int32(0), slot_count * lax.axis_size("seq")).astype(jnp.bfloat16),
        "seq",
        scatter_dimension=0,
        tiled=True,
    )
    shaped = summed.reshape(expert_count, capacity, -1)
    return lax.all_to_all(shaped, "exp", split_axis=0, concat_axis=0, tiled=True)


def per_device(
    resid_rows,
    query_rows,
    key_rows,
    value_rows,
    log_decay,
    read_pos,
    expert_ids,
    pair_order,
    lengths,
    norm_gain,
    router_weight,
    score_weight,
    gate_weight,
    up_weight,
    down_weight,
):
    seq_count = lax.axis_size("seq")
    exp_count = lax.axis_size("exp")
    seq_index = lax.axis_index("seq")
    exp_index = lax.axis_index("exp")
    token_count = key_rows.shape[1]
    model_width = key_rows.shape[2]
    head_count = log_decay.shape[1]
    head_size = model_width // head_count
    read_count = query_rows.shape[1]
    expert_count = router_weight.shape[1]
    capacity = max(2, 4 * read_count // exp_count)
    keys_half = key_rows[0].reshape(token_count, head_count, head_size)
    values_half = value_rows[0].reshape(token_count, head_count, head_size)
    query_half = query_rows[0].reshape(read_count, head_count, head_size)
    keys_float = keys_half.astype(jnp.float32)
    values_float = values_half.astype(jnp.float32)
    query_float = query_half.astype(jnp.float32)
    cumulated = jnp.cumsum(log_decay[0], axis=1)
    group_decay = jnp.exp(cumulated[:, -1])
    tail_decay = jnp.exp(cumulated[:, -1:] - cumulated).T[:, :, None]
    own_state = jnp.einsum("thi,thj->hij", keys_float * tail_decay, values_float, precision=PRECISE)
    state_in = chain_prefix(group_decay, own_state, False)
    places = read_pos[0] - seq_index * token_count
    at_read, weight = readout_weights(cumulated, places)
    lift = jnp.exp(at_read).T[:, :, None]
    query_key = (
        jnp.einsum("rhi,thi->hrt", query_half, keys_half, preferred_element_type=jnp.float32)
        / head_size
    )
    attended = jnp.einsum("hrt,thj->rhj", weight * query_key, values_float, precision=PRECISE)
    attended = (
        attended
        + lift * jnp.einsum("rhi,hij->rhj", query_float, state_in, precision=PRECISE) / head_size
    )
    residual = resid_rows[0].astype(jnp.float32) + attended.reshape(read_count, model_width)
    inverse = lax.rsqrt(jnp.mean(residual * residual, axis=1, keepdims=True) + EPSILON)
    unit_rows = residual * inverse
    gain_float = norm_gain.astype(jnp.float32)
    normed = (unit_rows * gain_float).astype(jnp.bfloat16)
    logits = jnp.dot(normed, router_weight, preferred_element_type=jnp.float32)
    picks = (
        expert_ids[0][:, :, None] == jnp.arange(expert_count, dtype=jnp.int32)[None, None, :]
    ).astype(jnp.float32)
    chosen = jnp.einsum("rke,re->rk", picks, logits, precision=PRECISE)
    first = jax.nn.sigmoid(chosen[:, 0] - chosen[:, 1])
    gates = jnp.stack([first, 1.0 - first], axis=1)
    flat = picks.reshape(read_count * 2, expert_count)
    earlier = jnp.cumsum(flat, axis=0) - flat
    slot_index = jnp.sum(earlier * flat, axis=1)
    slot_hot = (slot_index[:, None] == jnp.arange(capacity, dtype=jnp.float32)[None, :]).astype(
        jnp.float32
    )
    placement = (
        (flat[:, :, None] * slot_hot[:, None, :])
        .reshape(read_count * 2, expert_count * capacity)
        .astype(jnp.bfloat16)
    )
    doubled = jnp.repeat(normed, 2, axis=0)
    outgoing = jnp.dot(placement.T, doubled, preferred_element_type=jnp.float32).astype(
        jnp.bfloat16
    )
    arrived = to_experts(outgoing.reshape(expert_count, capacity, model_width)).reshape(
        expert_count * capacity, model_width
    )
    gate_w = gate_weight[0]
    up_w = up_weight[0]
    down_w = down_weight[0]
    hidden_count = gate_w.shape[1]

    def project_in(piece, start):
        gate_part = jnp.dot(piece, gate_w, preferred_element_type=jnp.float32)
        up_part = jnp.dot(piece, up_w, preferred_element_type=jnp.float32)
        return jnp.concatenate([gate_part, up_part], axis=1)

    projected = over_slots(arrived, project_in)
    pre_gate = projected[:, :hidden_count]
    pre_up = projected[:, hidden_count:]
    gate_sigmoid = jax.nn.sigmoid(pre_gate)
    activated = (pre_gate * gate_sigmoid * pre_up).astype(jnp.bfloat16)

    def project_out(start, count):
        return jnp.dot(activated, down_w, preferred_element_type=jnp.float32)

    returned = collect(project_out, expert_count, capacity)
    expert_out = jnp.dot(
        placement,
        returned.reshape(expert_count * capacity, model_width),
        preferred_element_type=jnp.float32,
    )
    expert_out = expert_out.reshape(read_count, 2, model_width)
    mixed = residual + jnp.sum(gates[:, :, None] * expert_out, axis=1)
    score_float = score_weight.astype(jnp.float32)
    score = jnp.dot(mixed, score_float, precision=PRECISE)
    own_total = jnp.sum(score) / (read_count * seq_count)
    seq_total = lax.psum(own_total, "seq")
    rewards = lax.all_gather(seq_total.reshape(1), "exp", axis=0, tiled=True)
    pair_loss, d_reward = jax.value_and_grad(preference_loss)(
        rewards, pair_order, lengths, token_count * seq_count
    )
    own_grad = jnp.sum(jnp.where(jnp.arange(exp_count) == exp_index, d_reward, 0.0)) * SCORE_SCALE
    d_mixed = jnp.broadcast_to((own_grad * score_float)[None, :], (read_count, model_width))
    d_out = (gates[:, :, None] * d_mixed[:, None, :]).astype(jnp.bfloat16)
    d_gates = jnp.einsum("rd,rkd->rk", d_mixed, expert_out, precision=PRECISE)
    d_logit = (d_gates[:, 0] - d_gates[:, 1]) * first * (1.0 - first)
    back_out = jnp.dot(
        placement.T, d_out.reshape(read_count * 2, model_width), preferred_element_type=jnp.float32
    ).astype(jnp.bfloat16)
    back_arrived = to_experts(back_out.reshape(expert_count, capacity, model_width)).reshape(
        expert_count * capacity, model_width
    )

    def project_back(piece, start):
        return jnp.einsum("sd,fd->sf", piece, down_w, preferred_element_type=jnp.float32)

    d_act = over_slots(back_arrived, project_back)
    d_pre_gate = (d_act * pre_up * gate_sigmoid * (1.0 + pre_gate * (1.0 - gate_sigmoid))).astype(
        jnp.bfloat16
    )
    d_pre_up = (d_act * pre_gate * gate_sigmoid).astype(jnp.bfloat16)

    def project_in_back(start, count):
        gate_term = jnp.einsum("sf,df->sd", d_pre_gate, gate_w, preferred_element_type=jnp.float32)
        up_term = jnp.einsum("sf,df->sd", d_pre_up, up_w, preferred_element_type=jnp.float32)
        return gate_term + up_term

    d_in_slots = collect(project_in_back, expert_count, capacity)
    d_in = jnp.dot(
        placement,
        d_in_slots.reshape(expert_count * capacity, model_width),
        preferred_element_type=jnp.float32,
    )
    d_in = d_in.reshape(read_count, 2, model_width)
    columns = jnp.einsum("rke,de->rkd", picks, router_weight.astype(jnp.float32), precision=PRECISE)
    d_normed = jnp.sum(d_in, axis=1) + d_logit[:, None] * (columns[:, 0] - columns[:, 1])
    d_unit = d_normed * gain_float
    grad_resid = d_mixed + inverse * (
        d_unit - unit_rows * jnp.mean(d_unit * unit_rows, axis=1, keepdims=True)
    )
    rounded = grad_resid.astype(jnp.bfloat16)
    d_half = rounded.reshape(read_count, head_count, head_size)
    d_attended = d_half.astype(jnp.float32)
    summary = (
        jnp.einsum("rhi,rhj->hij", query_float * lift, d_attended, precision=PRECISE) / head_size
    )
    suffix = chain_prefix(group_decay, summary, True)
    grad_dot = (
        jnp.einsum("rhj,thj->hrt", d_half, values_half, preferred_element_type=jnp.float32)
        / head_size
    )
    grad_query = jnp.einsum("hrt,thi->rhi", weight * grad_dot, keys_float, precision=PRECISE)
    grad_query = (
        grad_query
        + lift * jnp.einsum("rhj,hij->rhi", d_attended, state_in, precision=PRECISE) / head_size
    )
    grad_keys = jnp.einsum("hrt,rhi->thi", weight * grad_dot, query_float, precision=PRECISE)
    grad_keys = grad_keys + tail_decay * jnp.einsum(
        "hij,thj->thi", suffix, values_float, precision=PRECISE
    )
    grad_values = jnp.einsum("hrt,rhj->thj", weight * query_key, d_attended, precision=PRECISE)
    grad_values = grad_values + tail_decay * jnp.einsum(
        "thi,hij->thj", keys_float, suffix, precision=PRECISE
    )
    return (
        pair_loss,
        grad_query.reshape(1, read_count, model_width),
        grad_resid.reshape(1, read_count, model_width),
        grad_keys.reshape(1, token_count, model_width).astype(jnp.bfloat16),
        grad_values.reshape(1, token_count, model_width).astype(jnp.bfloat16),
    )


def solution(mesh):
    in_specs = (
        P("exp", "seq", None),
        P("exp", "seq", None),
        P("exp", "seq", None),
        P("exp", "seq", None),
        P("exp", None, "seq"),
        P("exp", "seq"),
        P("exp", "seq", None),
        P(),
        P(),
        P(),
        P(),
        P(),
        P("exp", None, "seq"),
        P("exp", None, "seq"),
        P("exp", "seq", None),
    )
    out_specs = (
        P(),
        P("exp", "seq", None),
        P("exp", "seq", None),
        P("exp", "seq", None),
        P("exp", "seq", None),
    )
    return jax.shard_map(
        per_device, mesh=mesh, in_specs=in_specs, out_specs=out_specs, check_vma=False
    )
```

profile of v0, /device:TPU:0, one launch (start us, length us, event | category | flops | bytes accessed | tf_op | source)
XLA Modules:
  0.0 582.2 jit_solution(4001827416699586467)
XLA Ops:
  7.2 1.6 copy.58
  9.9 2.3 fusion.28
  14.4 23.5 %all-reduce.2 = bf16[384]{0:T(512)(128)(2,1)S(1)} all-reduce(bf16[384]{0:T(512)(128)(2,1)S(1)} %dynamic-update-slice), channel_id=2, replica_groups=mesh['seq'=8,'exp'=4] {'seq'}, use_global_device_ids=true, to_apply=%add.2 | all-reduce | flops 384 | bytes 1536
  39.0 2.0 convolution_bitcast_fusion.3
  41.0 73.3 %all-gather.6.cloned.1.call-done = bf16[384,64,64]{2,1,0:T(8,128)(2,1)} async-done(((bf16[48,64,64]{2,1,0:T(8,128)(2,1)}), bf16[384,64,64]{2,1,0:T(8,128)(2,1)}) %all-gather.6.cloned.1.call-update) | async-done | bytes 3145744 | tf_op jit(solution)/shard_map/all_gather | solution.py:17
  114.5 1.8 multiply_reduce_fusion.1
  121.2 1.6 convolution_convert_fusion.1
  122.8 1.6 reshape.393
  124.3 8.3 %all_to_all.20 = bf16[4,4,3072]{2,1,0:T(4,128)(2,1)} all-to-all(bf16[4,4,3072]{2,1,0:T(4,128)(2,1)} %reshape.393), channel_id=1, replica_groups=mesh['seq'=8,'exp'=4] {'exp'}, dimensions={0} | all-to-all | bytes 196608 | tf_op jit(solution)/shard_map/all_to_all | solution.py:67
  132.6 1.6 reshape.394
  134.2 40.0 %all_gather.30 = bf16[128,3072]{1,0:T(8,128)(2,1)S(1)} all-gather(bf16[16,3072]{1,0:T(8,128)(2,1)} %reshape.394), channel_id=1, replica_groups=mesh['seq'=8,'exp'=4] {'seq'}, dimensions={0}, use_global_device_ids=true | all-gather | bytes 884736 | tf_op jit(solution)/shard_map/all_gather | solution.py:71
  174.2 4.4 fusion.6
  180.6 2.1 fusion.18
  194.2 51.5 %reduce-scatter.3.cloned.1.call-done = bf16[16,3072]{1,0:T(8,128)(2,1)} async-done(((bf16[128,3072]{1,0:T(8,128)(2,1)}), bf16[16,3072]{1,0:T(8,128)(2,1)}) %reduce-scatter.3.cloned.1.call-update) | async-done | bytes 98320 | tf_op jit(solution)/shard_map/reduce_scatter | solution.py:76
  245.7 1.6 reshape.395
  247.3 3.9 all-to-all-start.1
  253.9 1.7 all-to-all-done.1
  255.6 1.6 reshape.428
  257.2 1.7 multiply_reduce_fusion
  258.8 1.7 fusion.42
  261.1 20.5 %psum.7 = f32[1]{0:T(128)} all-reduce(f32[1]{0:T(128)} %bitcast.24), channel_id=1, replica_groups=mesh['seq'=8,'exp'=4] {'seq'}, use_global_device_ids=true, to_apply=%region_9.10 | all-reduce | flops 1 | bytes 8 | tf_op jit(solution)/shard_map/psum | solution.py:197
  282.2 2.4 dynamic-update-slice.1
  285.9 6.4 %all-reduce.3 = f32[4]{0:T(128)} all-reduce(f32[4]{0:T(128)} %dynamic-update-slice.1), channel_id=1, replica_groups=mesh['seq'=8,'exp'=4] {'exp'}, use_global_device_ids=true, to_apply=%add.3 | all-reduce | flops 4 | bytes 32
  294.9 2.0 fusion.100
  310.6 1.6 reshape.400
  312.2 8.3 %all_to_all.21 = bf16[4,4,3072]{2,1,0:T(4,128)(2,1)} all-to-all(bf16[4,4,3072]{2,1,0:T(4,128)(2,1)} %reshape.400), channel_id=1, replica_groups=mesh['seq'=8,'exp'=4] {'exp'}, dimensions={0} | all-to-all | bytes 196608 | tf_op jit(solution)/shard_map/all_to_all | solution.py:67
  320.5 1.6 reshape.401
  322.0 32.4 %all_gather.32 = bf16[128,3072]{1,0:T(8,128)(2,1)S(1)} all-gather(bf16[16,3072]{1,0:T(8,128)(2,1)} %reshape.401), channel_id=1, replica_groups=mesh['seq'=8,'exp'=4] {'seq'}, dimensions={0}, use_global_device_ids=true | all-gather | bytes 884736 | tf_op jit(solution)/shard_map/all_gather | solution.py:71
  354.5 5.5 fusion
  360.0 5.5 fusion.4
  365.6 3.3 fusion.15
  371.8 2.3 fusion.54
  375.4 52.4 %reduce-scatter.5.cloned.1.call-done = bf16[16,3072]{1,0:T(8,128)(2,1)} async-done(((bf16[128,3072]{1,0:T(8,128)(2,1)}), bf16[16,3072]{1,0:T(8,128)(2,1)}) %reduce-scatter.5.cloned.1.call-update) | async-done | bytes 98320 | tf_op jit(solution)/shard_map/reduce_scatter | solution.py:76
  427.8 1.6 reshape.402
  429.3 3.9 all-to-all-start.3
  436.0 1.6 all-to-all-done.3
  437.6 1.6 reshape.435
  439.2 1.7 convolution_reduce_fusion
  440.8 1.5 reduce_sum.123
  442.4 2.1 fusion.64
  448.5 3.1 multiply_convert_fusion
  460.6 2.9 fusion.73
  463.5 2.0 fusion.103
  466.3 82.6 %all-gather.8.cloned.1.call-done = bf16[384,64,64]{2,1,0:T(8,128)(2,1)} async-done(((bf16[48,64,64]{2,1,0:T(8,128)(2,1)}), bf16[384,64,64]{2,1,0:T(8,128)(2,1)}) %all-gather.8.cloned.1.call-update) | async-done | bytes 3145744 | tf_op jit(solution)/shard_map/all_gather | solution.py:17
  549.1 15.7 %while.27 = (s32[]{:T(128)}, f32[48,64,64]{2,1,0:T(8,128)S(1)}, s32[]{:T(128)}, bf16[8,48]{1,0:T(8,128)(2,1)}, bf16[8,48,64,64]{3,2,1,0:T(8,128)(2,1)}, /*index=5*/s32[]{:T(128)}, s32[]{:T(128)}, s32[]{:T(128)}, s32[]{:T(128)}) while((s32[]{:T(128)}, f32[48,64,64]{2,1,0:T(8,128)S(1)}, s32[]{:T(128)}, bf16[8,48]{1,0:T(8,128)(2,1)}, ...), condition=%wide.region_20.21_spmd, body=%wide.region_19.20_spmd.sunk | while | flops 589878 | bytes 1966715 | solution.py:32
  564.8 3.3 fusion.24
  568.2 2.3 copy.77
  570.5 2.9 fusion.22
  (186 shorter events, 74.7 us)
Async XLA Ops:
  7.2 182.8 %copy-start = (bf16[3072,4]{0,1:T(4,128)(2,1)S(1)}, bf16[3072,4]{0,1:T(4,128)(2,1)}, u32[]{:S(2)}) copy-start(bf16[3072,4]{0,1:T(4,128)(2,1)} %param.29) | copy-start | bytes 73732
  7.2 1.6 copy-start.5
  7.2 2.0 copy-start.23
  7.2 107.0 %all-gather.6.cloned.1.call-start = ((), (), s32[]{:S(2)}) async-start(), calls=%async_computation.8 | async-start | bytes 7077888 | tf_op jit(solution)/shard_map/all_gather | solution.py:17
  9.5 29.1 %copy-start.12 = (f32[48,128]{1,0:T(8,128)}, f32[48,128]{1,0:T(8,128)S(1)}, u32[]{:S(2)}) copy-start(f32[48,128]{1,0:T(8,128)S(1)} %reduce_window_sum.22) | copy-start | bytes 73732
  9.8 2.4 copy-start.27
  9.8 2.4 copy-start.14
  9.8 2.5 copy-start.33
  9.8 2.8 copy-start.26
  9.8 2.9 copy-start.34
  9.9 28.3 %copy-start.29 = (s32[1,4,2]{1,2,0:T(2,128)S(1)}, s32[1,4,2]{1,2,0:T(2,128)}, u32[]{:S(2)}) copy-start(s32[1,4,2]{1,2,0:T(2,128)} %param.25) | copy-start | bytes 100
  12.1 233.6 %reduce-scatter.3.cloned.1.call-start = ((), (), s32[]{:S(2)}) async-start(), calls=%async_computation.6 | async-start | bytes 884736 | tf_op jit(solution)/shard_map/reduce_scatter | solution.py:76
  12.6 101.8 %copy-start.24 = (f32[48,4]{1,0:T(8,128)}, f32[48,4]{1,0:T(8,128)S(1)}, u32[]{:S(2)}) copy-start(f32[48,4]{1,0:T(8,128)S(1)} %copy.57) | copy-start | bytes 2308
  38.1 76.3 %copy-start.10 = (f32[4,48]{0,1:T(8,128)}, f32[4,48]{0,1:T(8,128)S(1)}, u32[]{:S(2)}) copy-start(f32[4,48]{0,1:T(8,128)S(1)} %copy.61) | copy-start | bytes 2308
  38.6 75.8 %copy-start.35 = (pred[4,128]{1,0:T(4,128)(4,1)}, pred[4,128]{1,0:T(4,128)(4,1)S(1)}, u32[]{:S(2)}) copy-start(pred[4,128]{1,0:T(4,128)(4,1)S(1)} %iota_compare_fusion.4) | copy-start | bytes 1540
  39.0 75.2 %copy-start.16 = (f32[48,4,128]{2,1,0:T(4,128)}, f32[48,4,128]{2,1,0:T(4,128)S(1)}, u32[]{:S(2)}) copy-start(f32[48,4,128]{2,1,0:T(4,128)S(1)} %fusion.38) | copy-start | bytes 294916
  114.4 2.4 copy-start.32
  118.5 0.6 copy-start.22
  134.2 44.4 %slice-start = ((s8[7077888]{0:T(1024)(128)(4,1)}), s8[4194304]{0:T(1024)(128)(4,1)S(1)}, s32[]{:S(2)}) async-start(s8[7077888]{0:T(1024)(128)(4,1)} %bitcast.190), calls=%async_computation.10 | async-start | bytes 8388608
  134.2 46.4 %slice-start.4 = ((s8[7077888]{0:T(1024)(128)(4,1)}), s8[4194304]{0:T(1024)(128)(4,1)S(1)}, s32[]{:S(2)}) async-start(s8[7077888]{0:T(1024)(128)(4,1)} %bitcast.202), calls=%async_computation.14 | async-start | bytes 8388608
  174.2 4.4 slice-start.1
  174.2 6.4 %slice-start.5 = ((s8[7077888]{0:T(1024)(128)(4,1)}), s8[2883584]{0:T(1024)(128)(4,1)S(1)}, s32[]{:S(2)}) async-start(s8[7077888]{0:T(1024)(128)(4,1)} %bitcast.202), calls=%async_computation.15 | async-start | bytes 5767168
  178.6 1.2 copy-start.3
  179.8 0.8 copy-start.1
  247.3 8.3 %all-to-all-start.1 = ((bf16[4,4,3072]{2,1,0:T(4,128)(2,1)}), bf16[4,4,3072]{2,1,0:T(4,128)(2,1)}, u32[]{:S(2)}, u32[]{:S(2)}) async-start(bf16[4,4,3072]{2,1,0:T(4,128)(2,1)} %reshape.395), calls=%async_computation.2 | async-start | bytes 196608 | tf_op jit(solution)/shard_map/all_to_all | solution.py:83
  251.2 176.5 %reduce-scatter.5.cloned.1.call-start = ((), (), s32[]{:S(2)}) async-start(), calls=%async_computation.7 | async-start | bytes 884736 | tf_op jit(solution)/shard_map/reduce_scatter | solution.py:76
  308.6 0.6 copy-start.20
  354.5 5.5 copy-start.2
  354.5 11.1 %slice-start.2 = ((s8[7077888]{0:T(1024)(128)(4,1)}), s8[4194304]{0:T(1024)(128)(4,1)S(1)}, s32[]{:S(2)}) async-start(s8[7077888]{0:T(1024)(128)(4,1)} %bitcast.192), calls=%async_computation.12 | async-start | bytes 8388608
  360.0 5.6 slice-start.3
  360.0 5.6 copy-start.4
  368.9 70.3 %copy-start.28 = (bf16[4,2,16]{2,1,0:T(2,128)(2,1)S(1)}, bf16[4,2,16]{2,1,0:T(2,128)(2,1)}, u32[]{:S(2)}) copy-start(bf16[4,2,16]{2,1,0:T(2,128)(2,1)} %convert_element_type.214) | copy-start | bytes 772
  429.3 8.3 %all-to-all-start.3 = ((bf16[4,4,3072]{2,1,0:T(4,128)(2,1)}), bf16[4,4,3072]{2,1,0:T(4,128)(2,1)}, u32[]{:S(2)}, u32[]{:S(2)}) async-start(bf16[4,4,3072]{2,1,0:T(4,128)(2,1)} %reshape.402), calls=%async_computation.5 | async-start | bytes 196608 | tf_op jit(solution)/shard_map/all_to_all | solution.py:83
  433.3 115.7 %all-gather.8.cloned.1.call-start = ((), (), s32[]{:S(2)}) async-start(), calls=%async_computation.9 | async-start | bytes 7077888 | tf_op jit(solution)/shard_map/all_gather | solution.py:17
  447.8 0.6 copy-start.6
  448.5 6.9 %copy-start.13 = (f32[48,128]{1,0:T(8,128)S(1)}, f32[48,128]{1,0:T(8,128)}, u32[]{:S(2)}) copy-start(f32[48,128]{1,0:T(8,128)} %copy-done.12) | copy-start | bytes 73732
  448.5 6.9 %copy-start.25 = (f32[48,4]{1,0:T(8,128)S(1)}, f32[48,4]{1,0:T(8,128)}, u32[]{:S(2)}) copy-start(f32[48,4]{1,0:T(8,128)} %copy-done.24) | copy-start | bytes 2308
  451.6 6.8 %copy-start.7 = (bf16[4,48,64]{2,0,1:T(4,128)(2,1)S(1)}, bf16[4,48,64]{2,0,1:T(4,128)(2,1)}, u32[]{:S(2)}) copy-start(bf16[4,48,64]{2,0,1:T(4,128)(2,1)} %copy-done.6) | copy-start | bytes 73732
  451.6 6.8 %copy-start.11 = (f32[4,48]{0,1:T(8,128)S(1)}, f32[4,48]{0,1:T(8,128)}, u32[]{:S(2)}) copy-start(f32[4,48]{0,1:T(8,128)} %copy-done.10) | copy-start | bytes 2308
  456.4 0.7 copy-start.18
  459.8 3.7 copy-start.17
  460.5 5.0 copy-start.8
  460.5 5.0 copy-start.9
  460.5 5.0 copy-start.15
  460.5 5.0 copy-start.19
  460.5 5.0 copy-start.21
  460.5 5.0 copy-start.30
  460.6 5.0 copy-start.31
Sparse Core Ops, SparseCore 0:
  12.3 101.8 all-gather.5
  182.9 62.8 reduce-scatter.2
  369.0 58.6 reduce-scatter.4
  451.7 97.1 all-gather.7
where the time goes:
time: 585 us; the launch traced here: 582 us
  waiting for transfers between devices  263 us (45%)
  blocking collectives  139 us (24%)
  matrix products  62.9 us (11%)
  local copies, waits for them, and re-layouts  48.8 us (8%)
  other arithmetic  37.2 us (6%)
  between operations  22.4 us (4%)
  starting transfers between devices  8.01 us (1%)
    all_gather x2, waiting for transfers between devices, carried_in(): lax.all_gather(a.astype(kind), axis)  156 us
    reduce_scatter x2, waiting for transfers between devices, collect(): lax.psum_scatter(project(jnp.int32(0), slot_count * lax.axis_size('seq'))...  104 us
    all_gather x2, blocking collectives, over_slots(): lax.all_gather(arrived, 'seq', axis=0, tiled=True)  72.4 us
    unnamed x2, blocking collectives  29.9 us
    psum x1, blocking collectives, per_device(): seq_total = lax.psum(own_total, 'seq')  20.5 us
    all_to_all x2, blocking collectives, to_experts(): return lax.all_to_all(slots, 'exp', split_axis=0, concat_axis=0, tiled=True)  16.6 us
    unnamed x96, local copies, waits for them, and re-layouts  15.3 us
  transfers between devices with their start and end apart: 6, of which 6 were waited for; matrix products, arithmetic and copies ran while one was open for 7% of the time, Pallas kernels for 0%

commit v1 on v0

v1 whole, which is shorter than its diff:
```python
import functools

import jax
import jax.numpy as jnp
import numpy as np
from jax import lax
from jax.experimental import pallas as pl
from jax.experimental.pallas import tpu as pltpu
from jax.sharding import PartitionSpec as P

EPSILON = 1e-06
LENGTH_WEIGHT = 4.0
SCORE_SCALE = 256.0
NEGATIVE = -1e30
MESH = pl.DeviceIdType.MESH
F32 = jnp.float32
BF16 = jnp.bfloat16


def nt(a, b, **kw):
    return lax.dot_general(a, b, (((1,), (1,)), ((), ())), preferred_element_type=F32, **kw)


def tn(a, b):
    return lax.dot_general(a, b, (((0,), (0,)), ((), ())), preferred_element_type=F32)


def nn(a, b, **kw):
    return lax.dot_general(a, b, (((1,), (0,)), ((), ())), preferred_element_type=F32, **kw)


def iota(shape, dim):
    return lax.broadcasted_iota(jnp.int32, shape, dim)


def lane_sum(x):
    return jnp.sum(x, axis=1, keepdims=True)


def row_sum(x):
    return jnp.sum(x, axis=0, keepdims=True)


def tile_size(count, best):
    while count % best:
        best //= 2
    return best


def kernel(
    dims,
    q16_ref,
    rows_ref,
    key_ref,
    value_ref,
    decay_ref,
    pos_ref,
    ids_ref,
    order_ref,
    length_ref,
    rt_ref,
    gather_ref,
    spread_ref,
    merge_ref,
    gate_hbm,
    up_hbm,
    down_hbm,
    loss_ref,
    gquery_ref,
    gresid_ref,
    gkeys_ref,
    gvalues_ref,
    w_buf,
    down_buf,
    q_buf,
    info_buf,
    att_send,
    att_recv,
    n_buf,
    meta_buf,
    meta_exp,
    x_buf,
    acc,
    h_buf,
    act_buf,
    v_buf,
    u_buf,
    red_recv,
    red_sum,
    t_send,
    t_recv,
    seq_send,
    seq_recv,
    d_buf,
    gq_send,
    gq_recv,
    qn,
    dn,
    natural,
    w_scr,
    g_scr,
    send_sem,
    recv_sem,
    load_sem,
):
    S, E, R, D, H, TOK, F, Q = dims
    DQ, SR = D // Q, S * R
    NR = E * SR
    HD = D // H
    B = R * Q
    seq, exp = lax.axis_index("seq"), lax.axis_index("exp")
    seq_bits = [1 << b for b in range(S.bit_length() - 1)]
    exp_bits = [1 << b for b in range(E.bit_length() - 1)]
    used = [0]
    sent = []

    def flip(me, bit):
        return me + bit * (1 - 2 * ((me // bit) % 2))

    def push(src, dst, device):
        k = used[0]
        used[0] += 1
        copy = pltpu.make_async_remote_copy(
            src_ref=src,
            dst_ref=dst,
            send_sem=send_sem.at[k],
            recv_sem=recv_sem.at[k],
            device_id=device,
            device_id_type=MESH,
        )
        copy.start()
        sent.append(copy)
        return copy

    def rows_of(index, size):
        return pl.ds(pl.multiple_of(index * size, size), size)

    def share(buf, size):
        out = []
        for k in range(1, S):
            piece = buf.at[rows_of(seq, size)]
            out.append(push(piece, piece, (lax.rem(seq + k, S), exp)))
        return out

    def scatter(src, dst):
        out = []
        for k in range(1, S):
            to = lax.rem(seq + k, S)
            out.append(push(src.at[rows_of(to, B)], dst.at[rows_of(seq, B)], (to, exp)))
        return out

    def arrive(copies):
        for copy in copies:
            copy.wait_recv()

    loads = [
        pltpu.make_async_copy(down_hbm.at[0], down_buf, load_sem.at[0]),
        pltpu.make_async_copy(gate_hbm.at[0], w_buf.at[:, pl.ds(0, F)], load_sem.at[1]),
        pltpu.make_async_copy(up_hbm.at[0], w_buf.at[:, pl.ds(F, F)], load_sem.at[2]),
    ]
    for load in loads:
        load.start()

    barrier = pltpu.get_barrier_semaphore()
    peers = [(lax.rem(seq + k, S), exp) for k in range(1, S)]
    peers += [(seq, flip(exp, bit)) for bit in exp_bits]
    for peer in peers:
        pl.semaphore_signal(barrier, inc=1, device_id=peer, device_id_type=MESH)
    pl.semaphore_wait(barrier, len(peers))

    q_buf[rows_of(seq, B), :] = q16_ref[...]
    q_copies = share(q_buf, B)

    upper = (iota((TOK, TOK), 0) <= iota((TOK, TOK), 1)).astype(F32)
    cum = nn(decay_ref[0], upper, precision=lax.Precision.HIGHEST)
    sub8, lane8 = iota((8, TOK), 0), iota((8, TOK), 1)
    place = jnp.full((8, TOK), TOK - 1, jnp.int32)
    for r in range(R):
        place = jnp.where(sub8 == r, pos_ref[0, r] - seq * TOK, place)
    hot = (lane8 == place).astype(F32)
    marks = nt(hot, cum, precision=lax.Precision.HIGHEST)
    info_buf[rows_of(seq, 8), :] = jnp.zeros((8, 128), F32)
    info_buf[rows_of(seq, 8), 0:H] = marks
    info_copies = share(info_buf, 8)

    loads[0].wait()
    step = tile_size(F, 128)

    def project(i, carry):
        at = pl.multiple_of(i * step, step)
        v_buf[:, pl.ds(at, step)] = nt(rt_ref[...], down_buf[pl.ds(at, step), :])
        return carry

    lax.fori_loop(0, F // step, project, 0)

    arrive(info_copies)
    total = jnp.zeros((1, 128), F32)
    parts, masks = [], []
    lane_r, sub_r = iota((R, TOK), 1), iota((R, TOK), 0)
    own_place = jnp.zeros((R, TOK), jnp.int32)
    for r in range(R):
        own_place = jnp.where(sub_r == r, pos_ref[0, r] - seq * TOK, own_place)
    own_mask = jnp.where(lane_r <= own_place, 0.0, NEGATIVE)
    for j in range(S):
        block = info_buf[j * 8 : (j + 1) * 8, :]
        parts.append(block[0:R] + total)
        masks.append(jnp.where(j == seq, own_mask, jnp.where(j > seq, 0.0, NEGATIVE)))
        total = total + jnp.where(j >= seq, block[R : R + 1], 0.0)
    lifted = jnp.concatenate(parts, axis=0)
    mask = jnp.concatenate(masks, axis=0)

    arrive(q_copies)
    for c in range(Q):
        qn[:, c * DQ : (c + 1) * DQ] = nn(gather_ref[c], q_buf[...])

    group = 128 // HD
    lane = iota((SR, 128), 1)
    slots = [((lane >= g * HD) & (lane < (g + 1) * HD)) for g in range(group)]

    def stacked(x):
        return jnp.concatenate([jnp.where(s, x, 0.0) for s in slots], axis=0).astype(BF16)

    def chosen_lanes(x):
        out = x[0:SR]
        for g in range(1, group):
            out = jnp.where(slots[g], x[g * SR : (g + 1) * SR], out)
        return out

    for p in range(H // group):
        at = slice(p * 128, (p + 1) * 128)
        qk = nt(stacked(qn[:, at]), key_ref[0, :, at]) * (1.0 / HD)
        weight = jnp.concatenate(
            [
                jnp.exp(lifted[:, h : h + 1] - cum[h : h + 1, :] + mask)
                for h in range(p * group, (p + 1) * group)
            ],
            axis=0,
        )
        w_scr[p] = weight
        mixed = (weight * qk).astype(BF16)
        g_scr[p] = mixed
        natural[:, at] = chosen_lanes(nn(mixed, value_ref[0, :, at]))

    def to_blocks(dst):
        out = jnp.zeros((S * B, DQ), F32)
        for c in range(Q):
            out = out + nn(spread_ref[c], natural[:, c * DQ : (c + 1) * DQ].astype(BF16))
        dst[...] = out.astype(BF16)

    def from_blocks(buf):
        return jnp.concatenate([nn(merge_ref[c], buf[...]) for c in range(Q)], axis=1)

    to_blocks(att_send)
    copies = scatter(att_send, att_recv)
    att_recv[rows_of(seq, B), :] = att_send[rows_of(seq, B), :]
    arrive(copies)
    attended = from_blocks(att_recv)
    live = iota((8, 1), 0) < R
    residual = jnp.where(live, rows_ref[...] + attended, 0.0)
    gain = rows_ref[R : R + 1, :]
    score_w = rows_ref[R + 1 : R + 2, :]
    inverse = lax.rsqrt(lane_sum(residual * residual) * (1.0 / D) + EPSILON)
    unit = residual * inverse
    normed = jnp.concatenate([unit * gain, jnp.zeros((8, D), F32)], axis=0).astype(BF16)
    block = jnp.zeros((B, DQ), F32)
    pick = iota((B, 16), 0) - iota((B, 16), 1)
    low = iota((B, 16), 1) < R
    for c in range(Q):
        block = block + nn(
            ((pick == c * R) & low).astype(BF16), normed[:, c * DQ : (c + 1) * DQ]
        )
    n_buf[rows_of(seq, B), :] = block.astype(BF16)
    n_copies = share(n_buf, B)

    logits = nt(normed, rt_ref[...])[0:8]
    sub_l, lane_l = iota((8, 16), 0), iota((8, 16), 1)
    sub_n, lane_n = iota((8, NR), 0), iota((8, NR), 1)
    own_lane = (exp * S + seq) * R
    id0 = jnp.full((8, 16), -1, jnp.int32)
    id1 = jnp.full((8, 16), -1, jnp.int32)
    meta = jnp.zeros((8, NR), F32)
    for r in range(R):
        id0 = jnp.where(sub_l == r, ids_ref[0, r, 0], id0)
        id1 = jnp.where(sub_l == r, ids_ref[0, r, 1], id1)
        here = lane_n == own_lane + r
        meta = jnp.where(here & (sub_n == 0), ids_ref[0, r, 0].astype(F32), meta)
        meta = jnp.where(here & (sub_n == 1), ids_ref[0, r, 1].astype(F32), meta)
    difference = (lane_l == id0).astype(F32) - (lane_l == id1).astype(F32)
    first_own = jax.nn.sigmoid(lane_sum(difference * logits))
    base_own = lane_sum(residual * score_w)
    own_hot = (lane_n == own_lane + sub_n) & (sub_n < R)
    meta = meta + jnp.where(sub_n == 2, row_sum(jnp.where(own_hot, base_own, 0.0)), 0.0)
    meta = meta + jnp.where(sub_n == 3, row_sum(jnp.where(own_hot, first_own, 0.0)), 0.0)
    meta_buf[rows_of(seq, 8), :] = meta
    meta_copies = share(meta_buf, 8)

    arrive(n_copies)
    for c in range(Q):
        x_buf[c, rows_of(exp, SR), :] = nn(gather_ref[c], n_buf[...]).astype(BF16)
    downward = exp_bits[::-1]

    def spread_stage(c, bit):
        held = exp % (2 * bit)
        out = []
        for m in range(E // (2 * bit)):
            piece = x_buf.at[c, rows_of(held + m * 2 * bit, SR)]
            out.append(push(piece, piece, (seq, flip(exp, bit))))
        return out

    stage = [spread_stage(c, downward[0]) for c in range(Q)]
    arrive(meta_copies)
    meta = meta_buf[0:8, :]
    for j in range(1, S):
        meta = meta + meta_buf[j * 8 : (j + 1) * 8, :]

    for bit in downward[1:]:
        following = []
        for c in range(Q):
            arrive(stage[c])
            following.append(spread_stage(c, bit))
        stage = following

    for i, bit in enumerate(downward):
        meta_exp[2 * i] = meta
        copy = push(meta_exp.at[2 * i], meta_exp.at[2 * i + 1], (seq, flip(exp, bit)))
        copy.wait_recv()
        meta = meta + meta_exp[2 * i + 1]

    loads[1].wait()
    loads[2].wait()
    wide = tile_size(2 * F, 768 if (2 * F) % 768 == 0 else 256)
    for c in range(Q):
        arrive(stage[c])

        def grow(i, carry, c=c):
            at = pl.ds(pl.multiple_of(i * wide, wide), wide)
            part = nn(x_buf[c], w_buf[c * DQ : (c + 1) * DQ, at])
            acc[:, at] = part if c == 0 else acc[:, at] + part
            return carry

        lax.fori_loop(0, 2 * F // wide, grow, 0)

    id0_all, id1_all = meta[0:1], meta[1:2]
    base_all, first_all = meta[2:3], meta[3:4]
    mine = exp.astype(F32)
    gate_row = jnp.where(id0_all == mine, first_all, 0.0) + jnp.where(
        id1_all == mine, 1.0 - first_all, 0.0
    )
    v = v_buf[E : E + 1, :]
    sub16, lane16 = iota((16, NR), 0), iota((16, NR), 1)

    def activate(i, carry):
        at = pl.ds(pl.multiple_of(i * 16, 16), 16)
        gate = lane_sum(jnp.where(lane16 == sub16 + i * 16, gate_row, 0.0))
        pre_gate = acc[at, 0:F]
        pre_up = acc[at, F : 2 * F]
        sig = jax.nn.sigmoid(pre_gate)
        silu = pre_gate * sig
        act_buf[at, :] = (silu * pre_up).astype(BF16)
        gv = gate * v
        h_buf[at, 0:F] = (gv * pre_up * sig * (1.0 + pre_gate * (1.0 - sig))).astype(BF16)
        h_buf[at, F : 2 * F] = (gv * silu).astype(BF16)
        return carry

    lax.fori_loop(0, NR // 16, activate, 0)
    v_high = v.astype(BF16).astype(F32)
    sub_v = iota((16, F), 0)
    v_two = jnp.where(sub_v == 0, v_high, jnp.where(sub_v == 1, v - v_high, 0.0)).astype(BF16)
    own_t = row_sum(nt(v_two, act_buf[...]))
    table = jnp.where(sub_n == exp, own_t, 0.0)

    ladder = [(flip(seq, bit), exp) for bit in seq_bits] + [(seq, flip(exp, bit)) for bit in exp_bits]
    climb = []

    def climb_start(table):
        i = len(climb)
        t_send[i] = table
        climb.append(push(t_send.at[i], t_recv.at[i], ladder[i]))

    def climb_end(table):
        i = len(climb) - 1
        climb[i].wait_recv()
        return table + t_recv[i]

    offsets, count = [], E
    reach = 0
    for bit in exp_bits:
        offsets.append(reach)
        count //= 2
        reach += count * SR

    def held_rows(i, m):
        return u_buf, m * SR if i == 0 else offsets[i - 1] + m * SR

    def fold_start(c, i):
        bit = exp_bits[i]
        side = 1 - (exp // bit) % 2
        out = []
        for m in range(E // (2 * bit)):
            if i == 0:
                src = u_buf.at[c, rows_of(2 * m + side, SR)]
            else:
                src = red_sum.at[c, rows_of(offsets[i - 1] // SR + 2 * m + side, SR)]
            dst = red_recv.at[c, pl.ds(offsets[i] + m * SR, SR)]
            out.append(push(src, dst, (seq, flip(exp, bit))))
        return out

    def fold_end(c, i, copies):
        bit = exp_bits[i]
        side = (exp // bit) % 2
        for m, copy in enumerate(copies):
            copy.wait_recv()
            if i == 0:
                own = u_buf[c, rows_of(2 * m + side, SR), :]
            else:
                own = red_sum[c, rows_of(offsets[i - 1] // SR + 2 * m + side, SR), :]
            at = pl.ds(offsets[i] + m * SR, SR)
            red_sum[c, at, :] = (own.astype(F32) + red_recv[c, at, :].astype(F32)).astype(BF16)

    deep = tile_size(DQ, 256)
    folds = {}
    for c in range(Q):
        if c < len(ladder):
            climb_start(table)

        def back(i, carry, c=c):
            at = pl.multiple_of(i * deep, deep)
            u_buf[c, :, pl.ds(at, deep)] = nt(
                h_buf[...], w_buf[pl.ds(c * DQ + at, deep), :]
            ).astype(BF16)
            return carry

        lax.fori_loop(0, DQ // deep, back, 0)
        folds[c, 0] = fold_start(c, 0)
        if c >= 1:
            fold_end(c - 1, 0, folds[c - 1, 0])
            if len(exp_bits) > 1:
                folds[c - 1, 1] = fold_start(c - 1, 1)
        if c < len(ladder):
            table = climb_end(table)
    fold_end(Q - 1, 0, folds[Q - 1, 0])
    if len(exp_bits) > 1:
        folds[Q - 1, 1] = fold_start(Q - 1, 1)
    while len(climb) < len(ladder):
        climb_start(table)
        table = climb_end(table)

    low_e = iota((E, NR), 0).astype(F32)
    picked0 = row_sum(jnp.where(low_e == id0_all, table[0:E], 0.0))
    picked1 = row_sum(jnp.where(low_e == id1_all, table[0:E], 0.0))
    score = base_all + first_all * picked0 + (1.0 - first_all) * picked1
    in_seq = (lane_n >= sub_n * SR) & (lane_n < (sub_n + 1) * SR)
    rewards = lane_sum(jnp.where(in_seq, score, 0.0)) * (1.0 / SR)
    column = iota((8, 1), 0)
    d_reward = jnp.zeros((8, 1), F32)
    fitted = jnp.zeros((1, 1), F32)
    for pair in range(E // 2):
        best, worst = order_ref[2 * pair], order_ref[2 * pair + 1]
        gap = row_sum(
            jnp.where(column == worst, rewards, 0.0) - jnp.where(column == best, rewards, 0.0)
        )
        fitted = fitted + jnp.maximum(gap, 0.0) + jnp.log1p(jnp.exp(-jnp.abs(gap)))
        slope = jax.nn.sigmoid(gap) * (2.0 / E)
        d_reward = d_reward + jnp.where(column == worst, slope, 0.0)
        d_reward = d_reward - jnp.where(column == best, slope, 0.0)
    portion = jnp.zeros((8, 1), F32)
    for i in range(E):
        portion = jnp.where(column == i, length_ref[i].astype(F32) / (TOK * S), portion)
    real = column < E
    spread = jnp.where(real, portion - row_sum(portion) / E, 0.0)
    centred = jnp.where(real, rewards - row_sum(jnp.where(real, rewards, 0.0)) / E, 0.0)
    cov = row_sum(centred * spread) / E
    loss_ref[...] = jnp.broadcast_to(fitted * (2.0 / E) + LENGTH_WEIGHT * cov * cov, (8, 128))
    d_reward = d_reward + (2.0 * LENGTH_WEIGHT / E) * cov * spread
    own_grad = row_sum(jnp.where(column == exp, d_reward, 0.0)) * SCORE_SCALE
    d_logit_row = (picked0 - picked1) * first_all * (1.0 - first_all)
    d_logit = lane_sum(jnp.where(own_hot, d_logit_row, 0.0)) * own_grad

    for i in range(1, len(exp_bits)):
        for c in range(Q):
            fold_end(c, i, folds[c, i])
            if i + 1 < len(exp_bits):
                folds[c, i + 1] = fold_start(c, i + 1)
    out = jnp.zeros((S * B, DQ), F32)
    for c in range(Q):
        out = out + nn(spread_ref[c], red_sum[c, offsets[-1] : offsets[-1] + SR, :])
    seq_send[...] = out.astype(BF16)
    copies = scatter(seq_send, seq_recv)
    seq_recv[rows_of(seq, B), :] = seq_send[rows_of(seq, B), :]
    columns = nn(
        jnp.concatenate([difference, jnp.zeros((8, 16), F32)], axis=0).astype(BF16), rt_ref[...]
    )[0:8]
    arrive(copies)
    d_normed = own_grad * from_blocks(seq_recv) + d_logit * columns
    d_unit = d_normed * gain
    grad_resid = own_grad * score_w + inverse * (
        d_unit - unit * (lane_sum(d_unit * unit) * (1.0 / D))
    )
    grad_resid = jnp.where(live, grad_resid, 0.0)
    gresid_ref[0] = grad_resid[0:R]
    rounded = jnp.concatenate([grad_resid, jnp.zeros((8, D), F32)], axis=0).astype(BF16)
    block = jnp.zeros((B, DQ), F32)
    for c in range(Q):
        block = block + nn(
            ((pick == c * R) & low).astype(BF16), rounded[:, c * DQ : (c + 1) * DQ]
        )
    d_buf[rows_of(seq, B), :] = block.astype(BF16)
    arrive(share(d_buf, B))
    for c in range(Q):
        dn[:, c * DQ : (c + 1) * DQ] = nn(gather_ref[c], d_buf[...])

    for p in range(H // group):
        at = slice(p * 128, (p + 1) * 128)
        d_stack = stacked(dn[:, at])
        grad_dot = nt(d_stack, value_ref[0, :, at]) * (1.0 / HD)
        pulled = (w_scr[p] * grad_dot).astype(BF16)
        natural[:, at] = chosen_lanes(nn(pulled, key_ref[0, :, at]))
        gkeys_ref[0, :, at] = tn(pulled, stacked(qn[:, at])).astype(BF16)
        gvalues_ref[0, :, at] = tn(g_scr[p], d_stack).astype(BF16)
    to_blocks(gq_send)
    copies = scatter(gq_send, gq_recv)
    gq_recv[rows_of(seq, B), :] = gq_send[rows_of(seq, B), :]
    arrive(copies)
    gquery_ref[0] = from_blocks(gq_recv)[0:R]
    for copy in sent:
        copy.wait_send()


def per_device(
    resid_rows,
    query_rows,
    key_rows,
    value_rows,
    log_decay,
    read_pos,
    expert_ids,
    pair_order,
    lengths,
    norm_gain,
    router_weight,
    score_weight,
    gate_weight,
    up_weight,
    down_weight,
):
    S, E = lax.axis_size("seq"), lax.axis_size("exp")
    _, R, D = query_rows.shape
    TOK, H = key_rows.shape[1], log_decay.shape[1]
    F = gate_weight.shape[2]
    extra = -F % 128
    if extra:
        gate_weight = jnp.pad(gate_weight, ((0, 0), (0, 0), (0, extra)))
        up_weight = jnp.pad(up_weight, ((0, 0), (0, 0), (0, extra)))
        down_weight = jnp.pad(down_weight, ((0, 0), (0, extra), (0, 0)))
        F += extra
    Q = 16 // R
    B, DQ, SR = R * Q, D // Q, S * R
    NR = E * SR
    group = 128 // (D // H)

    gather = np.zeros((Q, SR, S * B), np.float32)
    merge = np.zeros((Q, 8, S * B), np.float32)
    for c in range(Q):
        for j in range(S):
            for r in range(R):
                gather[c, j * R + r, j * B + c * R + r] = 1
                merge[c, r, j * B + c * R + r] = 1
    spread = jnp.asarray(gather.transpose(0, 2, 1), BF16)
    gather, merge = jnp.asarray(gather, BF16), jnp.asarray(merge, BF16)

    q16 = query_rows[0].reshape(R, Q, DQ).transpose(1, 0, 2).reshape(B, DQ)
    rows = jnp.concatenate(
        [
            resid_rows[0].astype(F32),
            norm_gain.astype(F32)[None],
            score_weight.astype(F32)[None],
            jnp.zeros((8 - R - 2, D), F32),
        ],
        axis=0,
    )
    rt = jnp.concatenate(
        [router_weight.T, score_weight[None], jnp.zeros((16 - E - 1, D), BF16)], axis=0
    )

    stages = E.bit_length() - 1
    climbs = stages + S.bit_length() - 1
    sems = 8 * (S - 1) + 2 * Q * (E - 1) + stages + climbs
    vmem, smem, hbm = (
        pl.BlockSpec(memory_space=pltpu.VMEM),
        pl.BlockSpec(memory_space=pltpu.SMEM),
        pl.BlockSpec(memory_space=pl.ANY),
    )
    blocks = pltpu.VMEM((S * B, DQ), BF16)
    loss, gquery, gresid, gkeys, gvalues = pl.pallas_call(
        functools.partial(kernel, (S, E, R, D, H, TOK, F, Q)),
        out_shape=(
            jax.ShapeDtypeStruct((8, 128), F32),
            jax.ShapeDtypeStruct((1, R, D), F32),
            jax.ShapeDtypeStruct((1, R, D), F32),
            jax.ShapeDtypeStruct((1, TOK, D), BF16),
            jax.ShapeDtypeStruct((1, TOK, D), BF16),
        ),
        in_specs=[vmem] * 5 + [smem] * 4 + [vmem] * 4 + [hbm] * 3,
        out_specs=(vmem,) * 5,
        scratch_shapes=[
            pltpu.VMEM((D, 2 * F), BF16),
            pltpu.VMEM((F, D), BF16),
            blocks,
            pltpu.VMEM((S * 8, 128), F32),
            blocks,
            blocks,
            blocks,
            pltpu.VMEM((S * 8, NR), F32),
            pltpu.VMEM((2 * stages, 8, NR), F32),
            pltpu.VMEM((Q, NR, DQ), BF16),
            pltpu.VMEM((NR, 2 * F), F32),
            pltpu.VMEM((NR, 2 * F), BF16),
            pltpu.VMEM((NR, F), BF16),
            pltpu.VMEM((16, F), F32),
            pltpu.VMEM((Q, NR, DQ), BF16),
            pltpu.VMEM((Q, NR - SR, DQ), BF16),
            pltpu.VMEM((Q, NR - SR, DQ), BF16),
            pltpu.VMEM((climbs, 8, NR), F32),
            pltpu.VMEM((climbs, 8, NR), F32),
            blocks,
            blocks,
            blocks,
            blocks,
            blocks,
            pltpu.VMEM((SR, D), F32),
            pltpu.VMEM((SR, D), F32),
            pltpu.VMEM((SR, D), F32),
            pltpu.VMEM((H // group, group * SR, TOK), F32),
            pltpu.VMEM((H // group, group * SR, TOK), BF16),
            pltpu.SemaphoreType.DMA((sems,)),
            pltpu.SemaphoreType.DMA((sems,)),
            pltpu.SemaphoreType.DMA((3,)),
        ],
        compiler_params=pltpu.CompilerParams(
            collective_id=0, has_side_effects=True, vmem_limit_bytes=60 * 1024 * 1024
        ),
    )(
        q16,
        rows,
        key_rows,
        value_rows,
        log_decay,
        read_pos,
        expert_ids,
        pair_order,
        lengths,
        rt,
        gather,
        spread,
        merge,
        gate_weight,
        up_weight,
        down_weight,
    )
    return loss[0, 0], gquery, gresid, gkeys, gvalues


def solution(mesh):
    in_specs = (
        P("exp", "seq", None),
        P("exp", "seq", None),
        P("exp", "seq", None),
        P("exp", "seq", None),
        P("exp", None, "seq"),
        P("exp", "seq"),
        P("exp", "seq", None),
        P(),
        P(),
        P(),
        P(),
        P(),
        P("exp", None, "seq"),
        P("exp", None, "seq"),
        P("exp", "seq", None),
    )
    out_specs = (
        P(),
        P("exp", "seq", None),
        P("exp", "seq", None),
        P("exp", "seq", None),
        P("exp", "seq", None),
    )
    return jax.shard_map(
        per_device, mesh=mesh, in_specs=in_specs, out_specs=out_specs, check_vma=False
    )
```

time: 585 us -> 101 us (0.17)
  waiting for transfers between devices: 263 us -> 0 us
  blocking collectives: 139 us -> 0 us
  Pallas kernels: 0 us -> 83.7 us
  matrix products: 62.9 us -> 0 us
  local copies, waits for them, and re-layouts: 48.8 us -> 11.7 us
  other arithmetic: 37.2 us -> 4.31 us
  between operations: 22.4 us -> 0.65 us
  starting transfers between devices: 8.01 us -> 0 us
    all_gather x2 -> x0, waiting for transfers between devices: 156 us -> none  [carried_in(): lax.all_gather(a.astype(kind), axis)]
    reduce_scatter x2 -> x0, waiting for transfers between devices: 104 us -> none  [collect(): lax.psum_scatter(project(jnp.int32(0), slot_count * lax.axis_size('seq'))...]
    pallas_call x0 -> x1, Pallas kernels: none -> 83.7 us  [per_device(): pl.pallas_call(functools.partial(kernel, (S, E, R, D, H, TOK, F, Q)), out...]
    all_gather x2 -> x0, blocking collectives: 72.4 us -> none  [over_slots(): lax.all_gather(arrived, 'seq', axis=0, tiled=True)]
    dot_general x30 -> x0, matrix products: 62.9 us -> none  [the longest x1 5.53 us: project_in_back(): jnp.einsum('sf,df->sd', d_pre_up, up_w, preferred_element_type=jnp.float32)]
    unnamed x2 -> x0, blocking collectives: 29.9 us -> none
    psum x1 -> x0, blocking collectives: 20.5 us -> none  [per_device(): seq_total = lax.psum(own_total, 'seq')]
    reshape x14 -> x1, local copies, waits for them, and re-layouts: 18.7 us -> 1.36 us  [per_device(): q16 = query_rows[0].reshape(R, Q, DQ).transpose(1, 0, 2).reshape(B, DQ)]
  transfers between devices with their start and end apart: 6 -> 0, of which waited for: 6 -> 0; matrix products, arithmetic and copies ran while one was open for 7% -> 0% of each run, Pallas kernels for 0% -> 0%
where the time goes in v1:
time: 101 us; the launch traced here: 100 us
  Pallas kernels  83.7 us (83%)
  local copies, waits for them, and re-layouts  11.7 us (12%)
  other arithmetic  4.31 us (4%)
    pallas_call x1, Pallas kernels, per_device(): pl.pallas_call(functools.partial(kernel, (S, E, R, D, H, TOK, F, Q)), out...  83.7 us
    unnamed x5, local copies, waits for them, and re-layouts  8.3 us

profile of v1, /device:TPU:0, one launch (start us, length us, event | category | flops | bytes accessed | tf_op | source)
XLA Modules:
  0.0 100.4 jit_solution(16338204587161476844)
XLA Ops:
  0.6 0.1 pad.6.clone
  0.7 0.1 pad.2.clone
  0.8 1.3 %copy.24.ids_ref = s32[1,4,2]{2,1,0:T(4,128)} copy(s32[1,4,2]{1,2,0:T(2,128)} %param.24) | data formatting | bytes 64 | tf_op args[6]
  2.1 0.7 broadcast_in_dim.25
  2.8 0.7 reshape_convert_fusion
  3.5 0.7 broadcast_in_dim.21
  4.2 1.4 %reshape.15.q16_ref = bf16[16,768]{1,0:T(8,128)(2,1)} reshape(bf16[4,4,768]{2,1,0:T(4,128)(2,1)} %bitcast.10) | data formatting | bytes 49152 | tf_op jit(solution)/shard_map/reshape | solution.py:571
  5.6 0.7 bitcast_convert_fusion
  6.3 0.7 maximum_maximum_fusion.rows_ref
  7.0 1.5 %maximum_maximum_fusion.1.rt_ref = bf16[16,3072]{1,0:T(8,128)(2,1)} fusion(bf16[1,3072]{1,0:T(2,128)(2,1)S(1)} %broadcast_in_dim.21, bf16[4,3072]{1,0:T(4,128)(2,1)} %bitcast.11, bf16[16]{0:T(256)(128)(2,1)S(1)} %pad.2.clone), kind=kLoop, calls=%fused_computation.1 | loop fusion | flops 294912 | bytes 129056 | tf_op jit(solution)/shard_map/concatenate | solution.py:581
  8.5 83.7 %shard_map.209 = (f32[8,128]{1,0:T(8,128)}, f32[1,4,3072]{2,1,0:T(4,128)}, f32[1,4,3072]{2,1,0:T(4,128)}, bf16[1,128,3072]{2,1,0:T(8,128)(2,1)}, bf16[1,128,3072]{2,1,0:T(8,128)(2,1)}) custom-call(bf16[16,768]{1,0:T(8,128)(2,1)} %reshape.15.q16_ref, f32[8,3072]{1,0:T(8,128)} %maximum_maximum_fusion.rows_ref, bf16[1,128,3072]{2,1,0:T(8,128)(2,1)} %key_ref.1, ...), custom_call_target="tpu_custom_call" | custom-call | tf_op jit(solution)/shard_map/pallas_call | solution.py:594
  92.2 1.2 %slice.3 = f32[1,1]{1,0:T(1,128)} slice(f32[8,128]{1,0:T(8,128)} %get-tuple-element.10), slice={[0:1], [0:1]} | slice | bytes 8 | tf_op jit(solution)/shard_map/slice | solution.py:660
  93.4 1.4 %copy.29 = f32[1,4,3072]{2,1,0:T(4,128)} copy(f32[1,4,3072]{2,1,0:T(4,128)} %get-tuple-element.21) | data formatting | bytes 98304
  94.8 1.4 %copy.30 = f32[1,4,3072]{2,1,0:T(4,128)} copy(f32[1,4,3072]{2,1,0:T(4,128)} %get-tuple-element.22) | data formatting | bytes 98304
  96.2 2.1 %copy.31 = bf16[1,128,3072]{2,1,0:T(8,128)(2,1)} copy(bf16[1,128,3072]{2,1,0:T(8,128)(2,1)} %get-tuple-element.23) | data formatting | bytes 1572864
  98.3 2.1 %copy.32 = bf16[1,128,3072]{2,1,0:T(8,128)(2,1)} copy(bf16[1,128,3072]{2,1,0:T(8,128)(2,1)} %get-tuple-element.24) | data formatting | bytes 1572864
  (2 shorter events, 0.0 us)

commit v2 on v1

--- a/solution.py
+++ b/solution.py
@@ -12,6 +12,7 @@
 LENGTH_WEIGHT = 4.0
 SCORE_SCALE = 256.0
 NEGATIVE = -1e30
+PARTS = 2
 MESH = pl.DeviceIdType.MESH
 F32 = jnp.float32
 BF16 = jnp.bfloat16
@@ -49,8 +50,8 @@
 
 def kernel(
     dims,
-    q16_ref,
-    rows_ref,
+    query_ref,
+    resid_ref,
     key_ref,
     value_ref,
     decay_ref,
@@ -58,7 +59,9 @@
     ids_ref,
     order_ref,
     length_ref,
-    rt_ref,
+    gain_ref,
+    router_ref,
+    score_ref,
     gather_ref,
     spread_ref,
     merge_ref,
@@ -94,6 +97,11 @@
     d_buf,
     gq_send,
     gq_recv,
+    pad_query,
+    pad_resid,
+    pad_router,
+    rt_ref,
+    pulled_scr,
     qn,
     dn,
     natural,
@@ -105,6 +113,8 @@
 ):
     S, E, R, D, H, TOK, F, Q = dims
     DQ, SR = D // Q, S * R
+    DH = D // PARTS
+    DP = DH // Q
     NR = E * SR
     HD = D // H
     B = R * Q
@@ -137,17 +147,54 @@
 
     def share(buf, size):
         out = []
+        if size == B:
+            return [share_part(buf, h) for h in range(PARTS)]
         for k in range(1, S):
             piece = buf.at[rows_of(seq, size)]
             out.append(push(piece, piece, (lax.rem(seq + k, S), exp)))
         return out
 
-    def scatter(src, dst):
+    def share_part(buf, h):
+        out = []
+        for k in range(1, S):
+            piece = buf.at[h, rows_of(seq, B)]
+            out.append(push(piece, piece, (lax.rem(seq + k, S), exp)))
+        return out
+
+    def scatter(src, dst, h):
         out = []
         for k in range(1, S):
             to = lax.rem(seq + k, S)
-            out.append(push(src.at[rows_of(to, B)], dst.at[rows_of(seq, B)], (to, exp)))
+            out.append(push(src.at[h, rows_of(to, B)], dst.at[h, rows_of(seq, B)], (to, exp)))
+        dst[h, rows_of(seq, B), :] = src[h, rows_of(seq, B), :]
         return out
+
+    pick = iota((B, 16), 0) - iota((B, 16), 1)
+    low = iota((B, 16), 1) < R
+    picks = [((pick == c * R) & low).astype(BF16) for c in range(Q)]
+
+    def own_blocks(rows, buf):
+        for h in range(PARTS):
+            block = jnp.zeros((B, DP), F32)
+            for c in range(Q):
+                at = h * DH + c * DP
+                block = block + nn(picks[c], rows[:, at : at + DP])
+            buf[h, rows_of(seq, B), :] = block.astype(BF16)
+
+    def to_blocks(read, dst, h):
+        out = jnp.zeros((S * B, DP), F32)
+        for c in range(Q):
+            at = h * DH + c * DP
+            out = out + nn(spread_ref[c], read(slice(at, at + DP)).astype(BF16))
+        dst[h] = out.astype(BF16)
+
+    def from_blocks(buf, h):
+        return jnp.concatenate([nn(merge_ref[c], buf[h]) for c in range(Q)], axis=1)
+
+    def unpack(buf, dst, h):
+        for c in range(Q):
+            at = h * DH + c * DP
+            dst[:, at : at + DP] = nn(gather_ref[c], buf[h])
 
     def arrive(copies):
         for copy in copies:
@@ -166,11 +213,16 @@
     peers += [(seq, flip(exp, bit)) for bit in exp_bits]
     for peer in peers:
         pl.semaphore_signal(barrier, inc=1, device_id=peer, device_id_type=MESH)
-    pl.semaphore_wait(barrier, len(peers))
-
-    q_buf[rows_of(seq, B), :] = q16_ref[...]
-    q_copies = share(q_buf, B)
-
+
+    for ref in (pad_query, pad_resid, pad_router):
+        ref[...] = jnp.zeros(ref.shape, F32)
+    pad_query[0:R, :] = query_ref[0].astype(F32)
+    pad_resid[0:R, :] = resid_ref[0].astype(F32)
+    gain = gain_ref[...].astype(F32).reshape(1, D)
+    score_w = score_ref[...].astype(F32).reshape(1, D)
+    pad_router[0:E, :] = router_ref[...].astype(F32)
+    pad_router[E : E + 1, :] = score_w
+    rt_ref[...] = pad_router[...].astype(BF16)
     upper = (iota((TOK, TOK), 0) <= iota((TOK, TOK), 1)).astype(F32)
     cum = nn(decay_ref[0], upper, precision=lax.Precision.HIGHEST)
     sub8, lane8 = iota((8, TOK), 0), iota((8, TOK), 1)
@@ -181,7 +233,11 @@
     marks = nt(hot, cum, precision=lax.Precision.HIGHEST)
     info_buf[rows_of(seq, 8), :] = jnp.zeros((8, 128), F32)
     info_buf[rows_of(seq, 8), 0:H] = marks
+    own_blocks(pad_query[...].astype(BF16), q_buf)
+
+    pl.semaphore_wait(barrier, len(peers))
     info_copies = share(info_buf, 8)
+    q_copies = share(q_buf, B)
 
     loads[0].wait()
     step = tile_size(F, 128)
@@ -209,10 +265,6 @@
     lifted = jnp.concatenate(parts, axis=0)
     mask = jnp.concatenate(masks, axis=0)
 
-    arrive(q_copies)
-    for c in range(Q):
-        qn[:, c * DQ : (c + 1) * DQ] = nn(gather_ref[c], q_buf[...])
-
     group = 128 // HD
     lane = iota((SR, 128), 1)
     slots = [((lane >= g * HD) & (lane < (g + 1) * HD)) for g in range(group)]
@@ -226,50 +278,40 @@
             out = jnp.where(slots[g], x[g * SR : (g + 1) * SR], out)
         return out
 
+    heads = H // group // PARTS
     for p in range(H // group):
-        at = slice(p * 128, (p + 1) * 128)
-        qk = nt(stacked(qn[:, at]), key_ref[0, :, at]) * (1.0 / HD)
-        weight = jnp.concatenate(
+        w_scr[p] = jnp.concatenate(
             [
                 jnp.exp(lifted[:, h : h + 1] - cum[h : h + 1, :] + mask)
                 for h in range(p * group, (p + 1) * group)
             ],
             axis=0,
         )
-        w_scr[p] = weight
-        mixed = (weight * qk).astype(BF16)
-        g_scr[p] = mixed
-        natural[:, at] = chosen_lanes(nn(mixed, value_ref[0, :, at]))
-
-    def to_blocks(dst):
-        out = jnp.zeros((S * B, DQ), F32)
-        for c in range(Q):
-            out = out + nn(spread_ref[c], natural[:, c * DQ : (c + 1) * DQ].astype(BF16))
-        dst[...] = out.astype(BF16)
-
-    def from_blocks(buf):
-        return jnp.concatenate([nn(merge_ref[c], buf[...]) for c in range(Q)], axis=1)
-
-    to_blocks(att_send)
-    copies = scatter(att_send, att_recv)
-    att_recv[rows_of(seq, B), :] = att_send[rows_of(seq, B), :]
-    arrive(copies)
-    attended = from_blocks(att_recv)
+
+    att_copies = []
+    for part in range(PARTS):
+        arrive(q_copies[part])
+        unpack(q_buf, qn, part)
+        for p in range(part * heads, (part + 1) * heads):
+            at = slice(p * 128, (p + 1) * 128)
+            qk = nt(stacked(qn[:, at]), key_ref[0, :, at]) * (1.0 / HD)
+            mixed = (w_scr[p] * qk).astype(BF16)
+            g_scr[p] = mixed
+            natural[:, at] = chosen_lanes(nn(mixed, value_ref[0, :, at]))
+        to_blocks(lambda at: natural[:, at], att_send, part)
+        att_copies.append(scatter(att_send, att_recv, part))
+
+    attended = []
+    for part in range(PARTS):
+        arrive(att_copies[part])
+        attended.append(from_blocks(att_recv, part))
+    attended = jnp.concatenate(attended, axis=1)
     live = iota((8, 1), 0) < R
-    residual = jnp.where(live, rows_ref[...] + attended, 0.0)
-    gain = rows_ref[R : R + 1, :]
-    score_w = rows_ref[R + 1 : R + 2, :]
+    residual = jnp.where(live, pad_resid[...] + attended, 0.0)
     inverse = lax.rsqrt(lane_sum(residual * residual) * (1.0 / D) + EPSILON)
     unit = residual * inverse
     normed = jnp.concatenate([unit * gain, jnp.zeros((8, D), F32)], axis=0).astype(BF16)
-    block = jnp.zeros((B, DQ), F32)
-    pick = iota((B, 16), 0) - iota((B, 16), 1)
-    low = iota((B, 16), 1) < R
-    for c in range(Q):
-        block = block + nn(
-            ((pick == c * R) & low).astype(BF16), normed[:, c * DQ : (c + 1) * DQ]
-        )
-    n_buf[rows_of(seq, B), :] = block.astype(BF16)
+    own_blocks(normed, n_buf)
     n_copies = share(n_buf, B)
 
     logits = nt(normed, rt_ref[...])[0:8]
@@ -280,11 +322,11 @@
     id1 = jnp.full((8, 16), -1, jnp.int32)
     meta = jnp.zeros((8, NR), F32)
     for r in range(R):
-        id0 = jnp.where(sub_l == r, ids_ref[0, r, 0], id0)
-        id1 = jnp.where(sub_l == r, ids_ref[0, r, 1], id1)
+        id0 = jnp.where(sub_l == r, ids_ref[0, 0, r], id0)
+        id1 = jnp.where(sub_l == r, ids_ref[0, 1, r], id1)
         here = lane_n == own_lane + r
-        meta = jnp.where(here & (sub_n == 0), ids_ref[0, r, 0].astype(F32), meta)
-        meta = jnp.where(here & (sub_n == 1), ids_ref[0, r, 1].astype(F32), meta)
+        meta = jnp.where(here & (sub_n == 0), ids_ref[0, 0, r].astype(F32), meta)
+        meta = jnp.where(here & (sub_n == 1), ids_ref[0, 1, r].astype(F32), meta)
     difference = (lane_l == id0).astype(F32) - (lane_l == id1).astype(F32)
     first_own = jax.nn.sigmoid(lane_sum(difference * logits))
     base_own = lane_sum(residual * score_w)
@@ -294,9 +336,6 @@
     meta_buf[rows_of(seq, 8), :] = meta
     meta_copies = share(meta_buf, 8)
 
-    arrive(n_copies)
-    for c in range(Q):
-        x_buf[c, rows_of(exp, SR), :] = nn(gather_ref[c], n_buf[...]).astype(BF16)
     downward = exp_bits[::-1]
 
     def spread_stage(c, bit):
@@ -307,7 +346,17 @@
             out.append(push(piece, piece, (seq, flip(exp, bit))))
         return out
 
-    stage = [spread_stage(c, downward[0]) for c in range(Q)]
+    stage = []
+    per_part = DQ // DP
+    for h in range(PARTS):
+        arrive(n_copies[h])
+        for k in range(Q // PARTS):
+            c = h * (Q // PARTS) + k
+            for i in range(per_part):
+                x_buf[c, rows_of(exp, SR), i * DP : (i + 1) * DP] = nn(
+                    gather_ref[k * per_part + i], n_buf[h]
+                ).astype(BF16)
+            stage.append(spread_stage(c, downward[0]))
     arrive(meta_copies)
     meta = meta_buf[0:8, :]
     for j in range(1, S):
@@ -369,7 +418,8 @@
     own_t = row_sum(nt(v_two, act_buf[...]))
     table = jnp.where(sub_n == exp, own_t, 0.0)
 
-    ladder = [(flip(seq, bit), exp) for bit in seq_bits] + [(seq, flip(exp, bit)) for bit in exp_bits]
+    ladder = [(seq, flip(exp, bit)) for bit in exp_bits]
+    ladder += [(flip(seq, bit), exp) for bit in seq_bits]
     climb = []
 
     def climb_start(table):
@@ -470,28 +520,36 @@
     spread = jnp.where(real, portion - row_sum(portion) / E, 0.0)
     centred = jnp.where(real, rewards - row_sum(jnp.where(real, rewards, 0.0)) / E, 0.0)
     cov = row_sum(centred * spread) / E
-    loss_ref[...] = jnp.broadcast_to(fitted * (2.0 / E) + LENGTH_WEIGHT * cov * cov, (8, 128))
+    loss_ref[...] = fitted * (2.0 / E) + LENGTH_WEIGHT * cov * cov
     d_reward = d_reward + (2.0 * LENGTH_WEIGHT / E) * cov * spread
     own_grad = row_sum(jnp.where(column == exp, d_reward, 0.0)) * SCORE_SCALE
     d_logit_row = (picked0 - picked1) * first_all * (1.0 - first_all)
     d_logit = lane_sum(jnp.where(own_hot, d_logit_row, 0.0)) * own_grad
 
-    for i in range(1, len(exp_bits)):
-        for c in range(Q):
+    last = pl.ds(offsets[-1], SR)
+    copies = []
+    for c in range(Q):
+        for i in range(1, len(exp_bits)):
             fold_end(c, i, folds[c, i])
             if i + 1 < len(exp_bits):
                 folds[c, i + 1] = fold_start(c, i + 1)
-    out = jnp.zeros((S * B, DQ), F32)
-    for c in range(Q):
-        out = out + nn(spread_ref[c], red_sum[c, offsets[-1] : offsets[-1] + SR, :])
-    seq_send[...] = out.astype(BF16)
-    copies = scatter(seq_send, seq_recv)
-    seq_recv[rows_of(seq, B), :] = seq_send[rows_of(seq, B), :]
+        if (c + 1) % (Q // PARTS) == 0:
+            h = c // (Q // PARTS)
+
+            def reduced(at):
+                k = at.start // DQ
+                return red_sum[k, last, at.start - k * DQ : at.stop - k * DQ]
+
+            to_blocks(reduced, seq_send, h)
+            copies.append(scatter(seq_send, seq_recv, h))
     columns = nn(
         jnp.concatenate([difference, jnp.zeros((8, 16), F32)], axis=0).astype(BF16), rt_ref[...]
     )[0:8]
-    arrive(copies)
-    d_normed = own_grad * from_blocks(seq_recv) + d_logit * columns
+    pieces = []
+    for h in range(PARTS):
+        arrive(copies[h])
+        pieces.append(from_blocks(seq_recv, h))
+    d_normed = own_grad * jnp.concatenate(pieces, axis=1) + d_logit * columns
     d_unit = d_normed * gain
     grad_resid = own_grad * score_w + inverse * (
         d_unit - unit * (lane_sum(d_unit * unit) * (1.0 / D))
@@ -499,31 +557,42 @@
     grad_resid = jnp.where(live, grad_resid, 0.0)
     gresid_ref[0] = grad_resid[0:R]
     rounded = jnp.concatenate([grad_resid, jnp.zeros((8, D), F32)], axis=0).astype(BF16)
-    block = jnp.zeros((B, DQ), F32)
-    for c in range(Q):
-        block = block + nn(
-            ((pick == c * R) & low).astype(BF16), rounded[:, c * DQ : (c + 1) * DQ]
-        )
-    d_buf[rows_of(seq, B), :] = block.astype(BF16)
-    arrive(share(d_buf, B))
-    for c in range(Q):
-        dn[:, c * DQ : (c + 1) * DQ] = nn(gather_ref[c], d_buf[...])
-
+    own_blocks(rounded, d_buf)
+    d_copies = share(d_buf, B)
+    gq_copies = []
+    for part in range(PARTS):
+        arrive(d_copies[part])
+        unpack(d_buf, dn, part)
+        for p in range(part * heads, (part + 1) * heads):
+            at = slice(p * 128, (p + 1) * 128)
+            grad_dot = nt(stacked(dn[:, at]), value_ref[0, :, at]) * (1.0 / HD)
+            pulled = (w_scr[p] * grad_dot).astype(BF16)
+            pulled_scr[p] = pulled
+            natural[:, at] = chosen_lanes(nn(pulled, key_ref[0, :, at]))
+        to_blocks(lambda at: natural[:, at], gq_send, part)
+        gq_copies.append(scatter(gq_send, gq_recv, part))
     for p in range(H // group):
         at = slice(p * 128, (p + 1) * 128)
-        d_stack = stacked(dn[:, at])
-        grad_dot = nt(d_stack, value_ref[0, :, at]) * (1.0 / HD)
-        pulled = (w_scr[p] * grad_dot).astype(BF16)
-        natural[:, at] = chosen_lanes(nn(pulled, key_ref[0, :, at]))
-        gkeys_ref[0, :, at] = tn(pulled, stacked(qn[:, at])).astype(BF16)
-        gvalues_ref[0, :, at] = tn(g_scr[p], d_stack).astype(BF16)
-    to_blocks(gq_send)
-    copies = scatter(gq_send, gq_recv)
-    gq_recv[rows_of(seq, B), :] = gq_send[rows_of(seq, B), :]
-    arrive(copies)
-    gquery_ref[0] = from_blocks(gq_recv)[0:R]
+        gkeys_ref[0, :, at] = tn(pulled_scr[p], stacked(qn[:, at])).astype(BF16)
+        gvalues_ref[0, :, at] = tn(g_scr[p], stacked(dn[:, at])).astype(BF16)
+    for part in range(PARTS):
+        arrive(gq_copies[part])
+        gquery_ref[0, :, part * DH : (part + 1) * DH] = from_blocks(gq_recv, part)[0:R]
     for copy in sent:
         copy.wait_send()
+
+
+def hand_out(*refs):
+    sems = refs[-1]
+    copies = [
+        pltpu.make_async_copy(src, dst, sems.at[i])
+        for i, (src, dst) in enumerate(zip(refs[1:5], refs[6:10]))
+    ]
+    for copy in copies:
+        copy.start()
+    refs[5][...] = refs[0][...]
+    for copy in copies:
+        copy.wait()
 
 
 def per_device(
@@ -568,39 +637,25 @@
     spread = jnp.asarray(gather.transpose(0, 2, 1), BF16)
     gather, merge = jnp.asarray(gather, BF16), jnp.asarray(merge, BF16)
 
-    q16 = query_rows[0].reshape(R, Q, DQ).transpose(1, 0, 2).reshape(B, DQ)
-    rows = jnp.concatenate(
-        [
-            resid_rows[0].astype(F32),
-            norm_gain.astype(F32)[None],
-            score_weight.astype(F32)[None],
-            jnp.zeros((8 - R - 2, D), F32),
-        ],
-        axis=0,
-    )
-    rt = jnp.concatenate(
-        [router_weight.T, score_weight[None], jnp.zeros((16 - E - 1, D), BF16)], axis=0
-    )
-
     stages = E.bit_length() - 1
     climbs = stages + S.bit_length() - 1
-    sems = 8 * (S - 1) + 2 * Q * (E - 1) + stages + climbs
+    sems = (6 * PARTS + 2) * (S - 1) + 2 * Q * (E - 1) + stages + climbs
     vmem, smem, hbm = (
         pl.BlockSpec(memory_space=pltpu.VMEM),
         pl.BlockSpec(memory_space=pltpu.SMEM),
         pl.BlockSpec(memory_space=pl.ANY),
     )
-    blocks = pltpu.VMEM((S * B, DQ), BF16)
-    loss, gquery, gresid, gkeys, gvalues = pl.pallas_call(
+    blocks = pltpu.VMEM((PARTS, S * B, D // PARTS // Q), BF16)
+    results = pl.pallas_call(
         functools.partial(kernel, (S, E, R, D, H, TOK, F, Q)),
         out_shape=(
-            jax.ShapeDtypeStruct((8, 128), F32),
+            jax.ShapeDtypeStruct((1, 1), F32),
             jax.ShapeDtypeStruct((1, R, D), F32),
             jax.ShapeDtypeStruct((1, R, D), F32),
             jax.ShapeDtypeStruct((1, TOK, D), BF16),
             jax.ShapeDtypeStruct((1, TOK, D), BF16),
         ),
-        in_specs=[vmem] * 5 + [smem] * 4 + [vmem] * 4 + [hbm] * 3,
+        in_specs=[vmem] * 5 + [smem] * 4 + [vmem] * 6 + [hbm] * 3,
         out_specs=(vmem,) * 5,
         scratch_shapes=[
             pltpu.VMEM((D, 2 * F), BF16),
@@ -627,6 +682,11 @@
             blocks,
             blocks,
             blocks,
+            pltpu.VMEM((16, D), F32),
+            pltpu.VMEM((8, D), F32),
+            pltpu.VMEM((16, D), F32),
+            pltpu.VMEM((16, D), BF16),
+            pltpu.VMEM((H // group, group * SR, TOK), BF16),
             pltpu.VMEM((SR, D), F32),
             pltpu.VMEM((SR, D), F32),
             pltpu.VMEM((SR, D), F32),
@@ -640,16 +700,18 @@
             collective_id=0, has_side_effects=True, vmem_limit_bytes=60 * 1024 * 1024
         ),
     )(
-        q16,
-        rows,
+        query_rows,
+        resid_rows,
         key_rows,
         value_rows,
         log_decay,
         read_pos,
-        expert_ids,
+        expert_ids.transpose(0, 2, 1),
         pair_order,
         lengths,
-        rt,
+        norm_gain,
+        router_weight.T,
+        score_weight,
         gather,
         spread,
         merge,
@@ -657,7 +719,14 @@
         up_weight,
         down_weight,
     )
-    return loss[0, 0], gquery, gresid, gkeys, gvalues
+    moved = pl.pallas_call(
+        hand_out,
+        out_shape=tuple(jax.ShapeDtypeStruct(x.shape, x.dtype) for x in results),
+        in_specs=[vmem] + [hbm] * 4,
+        out_specs=(vmem,) + (hbm,) * 4,
+        scratch_shapes=[pltpu.SemaphoreType.DMA((4,))],
+    )(*results)
+    return (moved[0].reshape(()),) + tuple(moved[1:])
 
 
 def solution(mesh):

time: 101 us -> 130 us (1.29)
  Pallas kernels: 83.7 us -> 129 us
  local copies, waits for them, and re-layouts: 11.7 us -> 0 us
  other arithmetic: 4.31 us -> 0 us
    pallas_call x0 -> x1, Pallas kernels: none -> 52.9 us  [per_device(): pl.pallas_call(hand_out, out_shape=tuple((jax.ShapeDtypeStruct(x.shape, x...]
    unnamed x5 -> x0, local copies, waits for them, and re-layouts: 8.3 us -> none
    pallas_call x1, Pallas kernels: 83.7 us -> 76.5 us  [per_device(): pl.pallas_call(functools.partial(kernel, (S, E, R, D, H, TOK, F, Q)), out...]
    concatenate x2 -> x0, other arithmetic: 2.17 us -> none  [the longest x1 1.46 us: per_device(): jnp.concatenate([router_weight.T, score_weight[None], jnp.zeros((16 - E -...]
    broadcast_in_dim x2 -> x0, other arithmetic: 1.39 us -> none  [the longest x1 0.7 us: per_device(): score_weight.astype(F32)[None]]
    reshape x1 -> x0, local copies, waits for them, and re-layouts: 1.36 us -> none  [per_device(): q16 = query_rows[0].reshape(R, Q, DQ).transpose(1, 0, 2).reshape(B, DQ)]
where the time goes in v2:
time: 130 us
  Pallas kernels  129 us (99%)
    pallas_call x1, Pallas kernels, per_device(): pl.pallas_call(functools.partial(kernel, (S, E, R, D, H, TOK, F, Q)), out...  76.5 us
    pallas_call x1, Pallas kernels, per_device(): pl.pallas_call(hand_out, out_shape=tuple((jax.ShapeDtypeStruct(x.shape, x...  52.9 us

profile of v2, /device:TPU:0, one launch (start us, length us, event | category | flops | bytes accessed | tf_op | source)
XLA Modules:
  0.0 130.0 jit_solution(13950051282293673023)
XLA Ops:
  0.6 76.5 %shard_map.209 = (f32[1,1]{1,0:T(1,128)}, f32[1,4,3072]{2,1,0:T(4,128)}, f32[1,4,3072]{2,1,0:T(4,128)}, bf16[1,128,3072]{2,1,0:T(8,128)(2,1)}, bf16[1,128,3072]{2,1,0:T(8,128)(2,1)}) custom-call(bf16[1,4,3072]{2,1,0:T(4,128)(2,1)} %query_ref.1, bf16[1,4,3072]{2,1,0:T(4,128)(2,1)} %resid_ref.1, bf16[1,128,3072]{2,1,0:T(8,128)(2,1)} %key_ref.1, ...), custom_call_target="tpu_custom_call" | custom-call | tf_op jit(solution)/shard_map/pallas_call | solution.py:649
  77.1 52.9 %shard_map.210 = (f32[1,1]{1,0:T(1,128)}, f32[1,4,3072]{2,1,0:T(4,128)}, f32[1,4,3072]{2,1,0:T(4,128)}, bf16[1,128,3072]{2,1,0:T(8,128)(2,1)}, bf16[1,128,3072]{2,1,0:T(8,128)(2,1)}) custom-call(f32[1,1]{1,0:T(1,128)} %get-tuple-element.15.refs_0_, f32[1,4,3072]{2,1,0:T(4,128)} %get-tuple-element.16.refs_1_, f32[1,4,3072]{2,1,0:T(4,128)} %get-tuple-element.17.refs_2_, ...), custom_call_target="tpu_custom_call" | custom-call | tf_op jit(solution)/shard_map/pallas_call | solution.py:722
